TPU v7x, 256 devices: a whole 4x4x8 slice. The times are simulated.
256 devices in a mesh: rep: 4 (over z_hi, core), fsdp: 64 (over z_lo, x, y).
Axes of the slice: x: 4, y: 4, z: 8 (z_hi: 2, z_lo: 4; z = z_hi * 4 + z_lo), core: 2. Of those that a mesh axis runs over, the one named last changes fastest.
Arguments:
- grad_parts: bfloat16 [4, 16384, 8192], P('rep', 'fsdp'), may hold values from -6 to 6
- adam_m: float32 [4, 256, 8192], P('rep', 'fsdp'), may hold values from -16 to 16
- adam_v: float32 [4, 256, 8192], P('rep', 'fsdp'), may hold values from 1 to 10
- params_inner: float32 [4, 256, 8192], P('rep', 'fsdp'), may hold values from -3 to 3
- snapshot: float32 [256, 8192], P('fsdp'), may hold values from -1.5 to 1.5
- momentum: float32 [256, 8192], P('fsdp'), may hold values from -0.3 to 0.3
Outputs:
- adam_m_next: float32 [4, 256, 8192], P('rep', 'fsdp')
- adam_v_next: float32 [4, 256, 8192], P('rep', 'fsdp')
- params_next: float32 [256, 8192], P('fsdp', 'rep')
- momentum_next: float32 [256, 8192], P('fsdp', 'rep')
- weights: bfloat16 [256, 8192], replicated
All inputs are finite; a program needn't handle non-finite values. Where the computation divides by a largest or mean magnitude, that divisor is 1e-20 or more.
Results may differ from a plain program's by a relative error of at most 0.0095.
Values may be sent and summed in bfloat16 or wider, within the bound.
A program may use at most 64 MiB of HBM per device.

v0:
```python
import jax
import jax.numpy as jnp
from jax import lax
from jax.sharding import PartitionSpec as P

BLOCK = 128


def column_slice(values, col_start, width):
    return lax.dynamic_slice_in_dim(values, col_start, width, 1)


def whole_term(grad_rows):
    return grad_rows.astype(jnp.float32)


def inner_update(gradient, moment_one, moment_two, params_held, snap_held):
    moment_one_next = 0.9 * moment_one + 0.1 * gradient
    moment_two_next = 0.95 * moment_two + 0.05 * gradient * gradient
    update = moment_one_next / (jnp.sqrt(moment_two_next) + 1e-08)
    inner_params = params_held - 0.02 * (update + 0.1 * params_held)
    pseudo = snap_held - inner_params[0]
    return (moment_one_next, moment_two_next, pseudo)


def local(grad_parts, adam_m, adam_v, params_inner, snapshot, momentum):
    grad_rows = grad_parts[0]
    gradient = lax.psum_scatter(whole_term(grad_rows), "fsdp", scatter_dimension=0, tiled=True)[
        None
    ]
    adam_m_next, adam_v_next, pseudo = inner_update(
        gradient, adam_m, adam_v, params_inner, snapshot
    )
    row_peak = jnp.max(jnp.abs(pseudo), axis=1)
    row_count = pseudo.shape[0]
    block_count = row_count * lax.axis_size("fsdp") // BLOCK
    row_global = lax.axis_index("fsdp") * row_count + jnp.arange(row_count, dtype=jnp.int32)
    block_of = row_global // BLOCK
    in_block = block_of[:, None] == jnp.arange(block_count, dtype=jnp.int32)[None, :]
    local_peak = jnp.max(jnp.where(in_block, row_peak[:, None], 0.0), axis=0)
    peaks = lax.pmax(local_peak, "fsdp")
    row_limit = jnp.sum(jnp.where(in_block, peaks[None, :], 0.0), axis=1)
    factor = 0.5 / jnp.maximum(row_limit, 0.5)
    clipped = pseudo * factor[:, None]
    replicas = lax.axis_size("rep")
    width = pseudo.shape[1] // replicas
    col_start = lax.axis_index("rep") * width
    total = lax.psum(clipped.astype(jnp.bfloat16), "rep").astype(jnp.float32)
    averaged = total / replicas
    momentum_full = 0.9 * momentum + averaged
    params_full = snapshot - 0.7 * (averaged + 0.9 * momentum_full)
    weights = lax.all_gather(params_full.astype(jnp.bfloat16), "fsdp", axis=0, tiled=True)
    params_next = column_slice(params_full, col_start, width)
    momentum_next = column_slice(momentum_full, col_start, width)
    return (adam_m_next, adam_v_next, params_next, momentum_next, weights)


def solution(mesh):
    in_specs = (
        P("rep", "fsdp", None),
        P("rep", "fsdp", None),
        P("rep", "fsdp", None),
        P("rep", "fsdp", None),
        P("fsdp", None),
        P("fsdp", None),
    )
    out_specs = (
        P("rep", "fsdp", None),
        P("rep", "fsdp", None),
        P("fsdp", "rep"),
        P("fsdp", "rep"),
        P(),
    )
    return jax.shard_map(local, mesh=mesh, in_specs=in_specs, out_specs=out_specs, check_vma=False)
```

profile of v0, /device:TPU:8, one launch (start us, length us, event | category | flops | bytes accessed | tf_op | source)
XLA Modules:
  0.0 1360.2 jit_solution(3088992148531293077)
XLA Ops:
  7.2 0.0 copy-start.5
  7.2 0.0 copy-start
  7.2 0.0 copy-start.3
  7.2 0.0 copy-start.2
  7.2 0.0 copy-start.1
  7.2 0.0 copy-start.4
  7.2 0.0 all-reduce.6.cloned.1.call-start
  7.3 6.5 bitcast_convert_fusion
  13.8 0.0 all-reduce.6.cloned.1.call-update
  13.8 0.0 all-reduce.4.cloned.1.call-start
  13.9 0.0 copy-done.5
  13.9 0.6 dynamic-slice
  15.2 741.6 %all-reduce.6.cloned.1.call-done = f32[256,8192]{1,0:T(8,128)} async-done(((f32[256,8192]{1,0:T(8,128)}), f32[256,8192]{1,0:T(8,128)}) %all-reduce.6.cloned.1.call-update) | async-done | bytes 8388624
  756.8 0.0 copy-done
  756.8 0.0 copy-done.3
  756.8 0.0 copy-done.2
  756.8 0.0 copy-done.1
  756.8 2.0 abs_reduce_fusion
  758.8 0.1 select_reduce_fusion.1
  758.9 181.8 %pmax.7 = f32[2]{0:T(128)S(1)} all-reduce(f32[2]{0:T(128)S(1)} %select_reduce_fusion.1), channel_id=1, replica_groups=mesh['rep'=4,'fsdp'=64] {'fsdp'}, use_global_device_ids=true, to_apply=%region_3.4 | all-reduce | flops 2 | bytes 16 | tf_op jit(solution)/shard_map/pmax | solution.py:41
  940.7 0.1 select_reduce_fusion
  940.8 0.7 multiply_convert_fusion
  941.5 0.0 all-reduce.4.cloned.1.call-update
  941.5 0.0 all-gather.3.cloned.1.call-start
  941.6 53.5 %all-reduce.4.cloned.1.call-done = bf16[4,8192]{1,0:T(4,128)(2,1)} async-done(((bf16[4,8192]{1,0:T(4,128)(2,1)}), bf16[4,8192]{1,0:T(4,128)(2,1)}) %all-reduce.4.cloned.1.call-update) | async-done | bytes 65552 | tf_op jit(solution)/shard_map/psum | solution.py:48
  995.1 0.0 copy-done.4
  995.1 1.6 convert_bitcast_fusion
  996.7 0.0 all-gather.3.cloned.1.call-update
  996.7 0.6 constant_dynamic-slice_fusion
  997.3 349.5 %all-gather.3.cloned.1.call-done = bf16[64,4,8192]{2,1,0:T(4,128)(2,1)} async-done(((bf16[1,4,8192]{2,1,0:T(4,128)(2,1)}), bf16[64,4,8192]{2,1,0:T(4,128)(2,1)}) %all-gather.3.cloned.1.call-update) | async-done | bytes 4194320 | tf_op jit(solution)/shard_map/all_gather | solution.py:52
  1346.8 6.9 reshape.42
  (2 shorter events, 0.0 us)
Async XLA Ops:
  7.2 6.7 copy-start.5
  7.2 749.6 %copy-start = (f32[4,8192]{1,0:T(4,128)S(1)}, f32[4,8192]{1,0:T(4,128)}, u32[]{:S(2)}) copy-start(f32[4,8192]{1,0:T(4,128)} %param.10) | copy-start | bytes 393220
  7.2 749.6 %copy-start.3 = (f32[1,4,8192]{2,1,0:T(4,128)S(1)}, f32[1,4,8192]{2,1,0:T(4,128)}, u32[]{:S(2)}) copy-start(f32[1,4,8192]{2,1,0:T(4,128)} %param.7) | copy-start | bytes 393220
  7.2 749.6 %copy-start.2 = (f32[1,4,8192]{2,1,0:T(4,128)S(1)}, f32[1,4,8192]{2,1,0:T(4,128)}, u32[]{:S(2)}) copy-start(f32[1,4,8192]{2,1,0:T(4,128)} %param.8) | copy-start | bytes 393220
  7.2 749.6 %copy-start.1 = (f32[1,4,8192]{2,1,0:T(4,128)S(1)}, f32[1,4,8192]{2,1,0:T(4,128)}, u32[]{:S(2)}) copy-start(f32[1,4,8192]{2,1,0:T(4,128)} %param.9) | copy-start | bytes 393220
  7.2 987.9 %copy-start.4 = (f32[4,8192]{1,0:T(4,128)S(1)}, f32[4,8192]{1,0:T(4,128)}, u32[]{:S(2)}) copy-start(f32[4,8192]{1,0:T(4,128)} %param.11) | copy-start | bytes 393220
  7.2 749.6 %all-reduce.6.cloned.1.call-start = ((), (), s32[]{:S(2)}) async-start(), calls=%async_computation.2 | async-start | bytes 16777216
  13.8 981.2 %all-reduce.4.cloned.1.call-start = ((), (), s32[]{:S(2)}) async-start(), calls=%async_computation | async-start | bytes 131072 | tf_op jit(solution)/shard_map/psum | solution.py:48
  941.5 405.3 %all-gather.3.cloned.1.call-start = ((), (), s32[]{:S(2)}) async-start(), calls=%async_computation.1 | async-start | bytes 4259840 | tf_op jit(solution)/shard_map/all_gather | solution.py:52
Sparse Core Ops, SparseCore 0:
  14.0 742.7 all-reduce.5
  941.7 53.3 all-reduce.3
  997.6 349.1 all-gather.2
where the time goes:
time: 1360 us
  waiting for transfers between devices  1140 us (84%)
  blocking collectives  182 us (13%)
  between operations  14.5 us (1%)
    unnamed x4, waiting for transfers between devices  742 us
    all_gather x1, waiting for transfers between devices, local(): lax.all_gather(params_full.astype(jnp.bfloat16), 'fsdp', axis=0, tiled=True)  349 us
    pmax x1, blocking collectives, local(): peaks = lax.pmax(local_peak, 'fsdp')  182 us
    psum x1, waiting for transfers between devices, local(): total = lax.psum(clipped.astype(jnp.bfloat16), 'rep').astype(jnp.float32)  53.5 us
  transfers between devices with their start and end apart: 3, of which 3 were waited for; matrix products, arithmetic and copies ran while one was open for 0% of the time, Pallas kernels for 0%

commit v1 on v0

v1 whole, which is shorter than its diff:
```python
import functools

import jax
import jax.numpy as jnp
from jax import lax
from jax.experimental import pallas as pl
from jax.experimental.pallas import tpu as pltpu
from jax.sharding import PartitionSpec as P

D = 8192
K = 2
NR = 2 * K
W = D // NR
CW = W // 4
HW = CW // 2
NSEM = 200
F32 = jnp.float32
BF16 = jnp.bfloat16


def mo(v, m=128):
    return pl.multiple_of(v, m)


class Ring:
    def __init__(self, net, i, to_next, to_prev, raw, own, land, acc):
        self.net, self.i = net, i
        self.to_next, self.to_prev = to_next, to_prev
        self.raw, self.own, self.land, self.acc = raw, own, land, acc

    def start(self):
        i, net = self.i, self.net
        nxt, prv, far = (i + 1) % 4, (i + 3) % 4, (i + 2) % 4
        self.a = [
            net.send(self.raw(far, 0), self.land.at[0, 0], self.to_next),
            net.send(self.raw(far, 1), self.land.at[1, 0], self.to_prev),
        ]
        self.b = [
            net.send(self.raw(nxt, 1), self.land.at[0, 1], self.to_next),
            net.send(self.raw(prv, 0), self.land.at[1, 1], self.to_prev),
        ]

    def forward(self):
        i, net = self.i, self.net
        nxt, prv = (i + 1) % 4, (i + 3) % 4
        self.a[0].wait_recv()
        add(self.acc.at[0], [self.own(nxt, 0), self.land.at[0, 0]])
        c0 = net.send(self.acc.at[0], self.land.at[0, 2], self.to_next)
        self.a[1].wait_recv()
        add(self.acc.at[1], [self.own(prv, 1), self.land.at[1, 0]])
        c1 = net.send(self.acc.at[1], self.land.at[1, 2], self.to_prev)
        self.c = [c0, c1]

    def wait(self):
        for cp in self.b + self.c:
            cp.wait_recv()

    def terms(self, hh):
        land = self.land
        if hh == 0:
            return [self.own(self.i, 0), land.at[0, 2], land.at[1, 1]]
        return [self.own(self.i, 1), land.at[0, 1], land.at[1, 2]]


def add(dst, srcs):
    shape = dst.shape
    if len(shape) == 4:

        def body(j, _):
            dst[:, j] = functools.reduce(
                jnp.add, [s[:, j].astype(F32) for s in srcs]
            ).astype(BF16)
            return 0

        lax.fori_loop(0, shape[1], body, 0)
    else:

        def body(j, _):
            at = pl.ds(mo(j * 512, 512), 512)
            dst[:, :, at] = functools.reduce(
                jnp.add, [s[:, :, at].astype(F32) for s in srcs]
            ).astype(BF16)
            return 0

        lax.fori_loop(0, shape[2] // 512, body, 0)


class Net:
    def __init__(self, ss, rs):
        self.ss, self.rs, self.n = ss, rs, 0
        self.sent = []

    def send(self, src, dst, dev):
        n = self.n
        self.n += 1
        assert n < NSEM
        cp = pltpu.make_async_remote_copy(
            src, dst, self.ss.at[n], self.rs.at[n], device_id=dev
        )
        cp.start()
        self.sent.append(cp)
        return cp


def rows4(v, b):
    return v[4 * b : 4 * b + 4]


def kernel(
    grad, m_ref, v_ref, p_ref, snap, mom,
    m_out, v_out, pn_out, mn_out, w_out,
    G, LX1, LY1, AX1, AY1, SX1, SY1, L2, A2, M3, R3, Gs, PK, P1, P2, Pq, E, T, RT, Wb,
    ss, rs, ls,
):
    rep, f = lax.axis_index("rep"), lax.axis_index("fsdp")
    h, c = rep // 2, rep % 2
    z, x, y = f // 16, (f // 4) % 4, f % 4
    zp = z + 1 - 2 * (z % 2)
    Z = 4 * h + z

    def dev(h=h, c=c, z=z, x=x, y=y):
        return (2 * h + c, 16 * z + 4 * x + y)

    loc = []
    for r in range(NR):
        at = pl.ds(r * W, W)
        cp = pltpu.make_async_copy(grad.at[:, :, :, at], G.at[:, :, :, at], ls.at[r])
        cp.start()
        loc.append(cp)

    peers = [dev(x=(x + a) % 4, y=(y + b) % 4) for a in range(4) for b in range(4) if a or b]
    peers += [dev(z=(z + a) % 4, y=(y + b) % 4) for a in range(1, 4) for b in range(4)]
    peers += [dev(h=1 - h, z=(z + a) % 4) for a in range(4)]
    peers += [dev(h=hh, c=1 - c, z=zz) for hh in (h, 1 - h) for zz in (z, zp)]
    bar = pltpu.get_barrier_semaphore()
    for d in peers:
        pl.semaphore_signal(bar, 1, device_id=d)
    pl.semaphore_wait(bar, len(peers))

    net = Net(ss, rs)
    xn, xp = dev(x=(x + 1) % 4), dev(x=(x + 3) % 4)
    yn, yp = dev(y=(y + 1) % 4), dev(y=(y + 3) % 4)

    def first(r):
        k = r // 2
        if r % 2 == 0:

            def chunk(src, j, hh):
                return src.at[pl.ds(2 * hh, 2), j, :, pl.ds(r * W, W)]

            return Ring(
                net, x, xn, xp, functools.partial(chunk, grad), functools.partial(chunk, G),
                LX1.at[k], AX1.at[k],
            )

        def chunk(src, j, hh):
            return src.at[pl.ds(2 * hh, 2), :, :, pl.ds(mo(r * W + j * CW), CW)]

        return Ring(
            net, y, yn, yp, functools.partial(chunk, grad), functools.partial(chunk, G),
            LY1.at[k], AY1.at[k],
        )

    def second(r):
        k = r // 2
        if r % 2 == 0:

            def chunk(j, hh):
                return SX1.at[k].at[pl.ds(2 * hh, 2), :, pl.ds(mo(j * CW), CW)]

            return Ring(net, y, yn, yp, chunk, chunk, L2.at[r], A2.at[r])

        def chunk(j, hh):
            return SY1.at[k].at[pl.ds(2 * hh, 2), j]

        return Ring(net, x, xn, xp, chunk, chunk, L2.at[r], A2.at[r])

    one = [first(r) for r in range(NR)]
    two = [second(r) for r in range(NR)]

    def finish_first(k):
        for r in (2 * k, 2 * k + 1):
            one[r].wait()
            dst = (SX1 if r % 2 == 0 else SY1).at[k]
            for hh in range(2):
                add(dst.at[pl.ds(2 * hh, 2)], one[r].terms(hh))
        for r in (2 * k, 2 * k + 1):
            two[r].start()

    def finish_second(k):
        rings = two[2 * k], two[2 * k + 1]
        for ring in rings:
            ring.wait()
        for zz in range(4):
            halves = []
            for ring in rings:
                s = functools.reduce(
                    jnp.add, [t[zz % 2].astype(F32) for t in ring.terms(zz // 2)]
                )
                halves += [s[:, :HW], s[:, HW:]]
            for yy in range(4):
                M3[k, zz, yy] = jnp.concatenate([rows4(s, yy) for s in halves], 0).astype(BF16)
        return [
            net.send(
                M3.at[k, (z + dz) % 4, (y + dy) % 4],
                R3.at[k, dz, dy],
                dev(z=(z + dz) % 4, y=(y + dy) % 4),
            )
            for dz in (2, 1, 3, 0)
            for dy in range(4)
            if dz or dy
        ]

    one[0].start()
    one[1].start()
    one[2].start()
    one[3].start()
    for cp in loc:
        cp.wait()
    one[0].forward()
    one[1].forward()
    finish_first(0)
    one[2].forward()
    one[3].forward()
    two[0].forward()
    two[1].forward()
    third = finish_second(0)
    finish_first(1)
    two[2].forward()
    two[3].forward()
    third += finish_second(1)
    for cp in third:
        cp.wait_recv()

    for k in range(K):
        for dy in range(4):
            g = None
            for dz in range(4):
                t = (R3[k, dz, dy] if dz or dy else M3[k, z, y]).astype(F32)
                g = t if g is None else g + t
            ys = (y + 4 - dy) % 4
            for s in range(2):
                for t in range(2):
                    at = pl.ds(mo((2 * k + s) * W + ys * CW + t * HW), HW)
                    Gs[:, at] = rows4(g, 2 * s + t)

    top = None
    for q in range(4):
        parts = []
        for t in range(4):
            at = pl.ds(q * 2048 + t * 512, 512)
            g, params = Gs[:, at], p_ref[:, at]
            m_next = 0.9 * m_ref[:, at] + 0.1 * g
            v_next = 0.95 * v_ref[:, at] + 0.05 * g * g
            m_out[:, at] = m_next
            v_out[:, at] = v_next
            inner = params - 0.02 * (m_next / (jnp.sqrt(v_next) + 1e-8) + 0.1 * params)
            pseudo = snap[:, at] - inner
            parts.append(pseudo)
            size = jnp.abs(pseudo)
            top = size if top is None else jnp.maximum(top, size)
        Pq[q] = jnp.concatenate(parts, 0).astype(BF16)
    tile = functools.reduce(jnp.maximum, [top[:, 128 * i : 128 * i + 128] for i in range(4)])
    PK[0] = jnp.concatenate([tile, tile], 0)

    got = [
        net.send(PK.at[0], P1.at[4 * a + b], dev(x=(x + a) % 4, y=(y + b) % 4))
        for a in range(4)
        for b in range(4)
        if a or b
    ]

    def flip(dr):
        return (1 - h if dr // 2 else h), (1 - c if dr % 2 else c)

    sent_e = []
    for dr in (3, 2, 1):
        h2, c2 = flip(dr)
        sent_e.append(net.send(Pq.at[2 * h2 + c2], E.at[dr], dev(h=h2, c=c2)))
    peak = PK[0]
    for cp in got:
        cp.wait_recv()
    for i in range(1, 16):
        peak = jnp.maximum(peak, P1[i])
    PK[1] = peak
    got = []
    for dr in (3, 2, 1, 0):
        h2, c2 = flip(dr)
        for e in (1, 0):
            if dr or e:
                got.append(
                    net.send(PK.at[1], P2.at[e, dr], dev(h=h2, c=c2, z=zp if e else z))
                )
    for cp in got + sent_e:
        cp.wait_recv()
    total = None
    for dr in range(4):
        high = jnp.maximum(P2[0, dr] if dr else peak, P2[1, dr])
        high = jnp.max(high, axis=(0, 1), keepdims=True)
        factor = 0.5 / jnp.maximum(high, 0.5)
        term = (E[dr] if dr else Pq[rep]).astype(F32) * factor
        total = term if total is None else total + term
    averaged = total / 4
    new = []
    for t in range(4):
        avg = rows4(averaged, t)
        at = pl.ds(mo(rep * 2048 + t * 512), 512)
        m_new = 0.9 * mom[:, at] + avg
        p_new = snap[:, at] - 0.7 * (avg + 0.9 * m_new)
        mn_out[:, pl.ds(t * 512, 512)] = m_new
        pn_out[:, pl.ds(t * 512, 512)] = p_new
        new.append(p_new)
    new = jnp.concatenate(new, 1)
    for yy in range(4):
        pieces = [
            new[:, p * 1024 + yy * 256 + t * 128 : p * 1024 + yy * 256 + t * 128 + 128]
            for p in range(2)
            for t in range(2)
        ]
        T[yy] = jnp.concatenate(pieces, 0).astype(BF16)
    got = [
        net.send(T.at[(y + d) % 4], RT.at[y], dev(y=(y + d) % 4)) for d in (2, 1, 3)
    ]
    RT[y] = T[y]
    for cp in got:
        cp.wait_recv()
    for p in range(2):
        for t in range(2):
            b = 2 * p + t
            Wb[p, :, pl.ds(t * 128, 128)] = jnp.concatenate(
                [rows4(RT[ys].astype(F32), b) for ys in range(4)], 0
            ).astype(BF16)

    def small(p):
        return w_out.at[z, x, :, pl.ds(mo((2 * h + c) * 2048 + p * 1024 + y * 256), 256)]

    for p in range(2):
        cp = pltpu.make_async_copy(Wb.at[p], small(p), ls.at[p])
        cp.start()
        loc[p] = cp
    got = []
    for d in (4, 3, 5, 2, 6, 1, 7):
        Z2 = (Z + d) % 8
        for p in range(2):
            got.append(net.send(Wb.at[p], small(p), dev(h=Z2 // 4, z=Z2 % 4)))
    for p in range(2):
        loc[p].wait()
    for cp in got:
        cp.wait_recv()
    got = []
    for d in (2, 1, 3):
        for p, to in ((0, dev(y=(y + d) % 4)), (1, dev(x=(x + d) % 4))):
            for hh in range(2):
                blk = w_out.at[
                    :, x, :, pl.ds(mo((2 * hh + c) * 2048 + p * 1024 + y * 256), 256)
                ]
                got.append(net.send(blk, blk, to))
    for cp in got:
        cp.wait_recv()

    def large(p, i, hh):
        if p == 0:
            return w_out.at[:, i, :, pl.ds(mo((2 * hh + c) * 2048), 1024)]
        return w_out.at[:, :, :, pl.ds(mo((2 * hh + c) * 2048 + 1024 + i * 256), 256)]

    ways = ((x, xn, xp), (y, yn, yp))
    near = []
    for hh in range(2):
        for p, (i, nx, pv) in enumerate(ways):
            right = net.send(large(p, i, hh), large(p, i, hh), nx)
            left = net.send(large(p, i, 1 - hh), large(p, i, 1 - hh), pv)
            near.append((p, hh, right, left))
    sib = dev(c=1 - c)
    swaps = []

    def swap(p, i, hh):
        swaps.append(net.send(large(p, i, hh), large(p, i, hh), sib))

    for p, (i, _, _) in enumerate(ways):
        for hh in range(2):
            swap(p, i, hh)
    far = []
    for p, hh, right, left in near:
        i, nx, pv = ways[p]
        right.wait_recv()
        prv, nxt = (i + 3) % 4, (i + 1) % 4
        if hh == 0:
            far.append((p, 0, net.send(large(p, prv, 0), large(p, prv, 0), nx)))
        swap(p, prv, hh)
        left.wait_recv()
        if hh == 0:
            far.append((p, 1, net.send(large(p, nxt, 1), large(p, nxt, 1), pv)))
        swap(p, nxt, 1 - hh)
    for p, hh, cp in far:
        cp.wait_recv()
        swap(p, (ways[p][0] + 2) % 4, hh)
    for cp in swaps:
        cp.wait_recv()
    for cp in net.sent:
        cp.wait_send()


def local(grad_parts, adam_m, adam_v, params_inner, snapshot, momentum):
    vmem = pl.BlockSpec(memory_space=pltpu.VMEM)
    hbm = pl.BlockSpec(memory_space=pl.ANY)
    V = pltpu.VMEM
    m, v, pn, mn, w = pl.pallas_call(
        kernel,
        out_shape=(
            jax.ShapeDtypeStruct((4, D), F32),
            jax.ShapeDtypeStruct((4, D), F32),
            jax.ShapeDtypeStruct((4, 2048), F32),
            jax.ShapeDtypeStruct((4, 2048), F32),
            jax.ShapeDtypeStruct((4, 4, 16, D), BF16),
        ),
        in_specs=[hbm] + [vmem] * 5,
        out_specs=(vmem, vmem, vmem, vmem, hbm),
        scratch_shapes=[
            V((4, 4, 16, D), BF16),
            V((K, 2, 3, 2, 16, W), BF16),
            V((K, 2, 3, 2, 4, 16, CW), BF16),
            V((K, 2, 2, 16, W), BF16),
            V((K, 2, 2, 4, 16, CW), BF16),
            V((K, 4, 16, W), BF16),
            V((K, 4, 4, 16, CW), BF16),
            V((NR, 2, 3, 2, 16, CW), BF16),
            V((NR, 2, 2, 16, CW), BF16),
            V((K, 4, 4, 16, HW), BF16),
            V((K, 4, 4, 16, HW), BF16),
            V((4, D), F32),
            V((2, 8, 128), F32),
            V((16, 8, 128), F32),
            V((2, 4, 8, 128), F32),
            V((4, 16, 512), BF16),
            V((4, 16, 512), BF16),
            V((4, 16, 128), BF16),
            V((4, 16, 128), BF16),
            V((2, 16, 256), BF16),
            pltpu.SemaphoreType.DMA((NSEM,)),
            pltpu.SemaphoreType.DMA((NSEM,)),
            pltpu.SemaphoreType.DMA((8,)),
        ],
        compiler_params=pltpu.CompilerParams(
            collective_id=0, has_side_effects=True, vmem_limit_bytes=40 * 2**20
        ),
        name="outer_step",
    )(
        grad_parts.reshape(4, 4, 16, D),
        adam_m[0],
        adam_v[0],
        params_inner[0],
        snapshot,
        momentum,
    )
    return m[None], v[None], pn, mn, w.reshape(256, D)


def solution(mesh):
    rows = P("rep", "fsdp", None)
    flat = P("fsdp", None)
    return jax.shard_map(
        local,
        mesh=mesh,
        in_specs=(rows, rows, rows, rows, flat, flat),
        out_specs=(rows, rows, P("fsdp", "rep"), P("fsdp", "rep"), P()),
        check_vma=False,
    )
```

time: 1360 us -> 99.8 us (0.07)
  the two profiles are of different devices: /device:TPU:8 before, /device:TPU:1 now
where the time goes in v1:
time: 99.8 us; the launch traced here: 99.6 us
  Pallas kernels  87.7 us (88%)
  local copies, waits for them, and re-layouts  11.3 us (11%)
    pallas_call x1, Pallas kernels, local(): pl.pallas_call(kernel, out_shape=(jax.ShapeDtypeStruct((4, D), F32), jax....  87.7 us
    unnamed x17, local copies, waits for them, and re-layouts  11.3 us

profile of v1, /device:TPU:1, one launch (start us, length us, event | category | flops | bytes accessed | tf_op | source)
XLA Modules:
  0.0 99.6 jit_solution(1862257267455834154)
XLA Ops:
  0.6 0.0 copy-start
  0.6 2.2 %copy-done = bf16[1,256,8192]{2,1,0:T(8,128)(2,1)S(1)} copy-done((bf16[1,256,8192]{2,1,0:T(8,128)(2,1)S(1)}, bf16[1,256,8192]{2,1,0:T(8,128)(2,1)}, u32[]{:S(2)}) %copy-start) | copy-done | bytes 4194328
  2.8 0.0 copy-start.1
  2.8 0.9 copy-done.1
  3.7 0.0 copy-start.2
  3.7 0.9 copy-done.2
  4.6 0.0 copy-start.3
  4.6 0.9 copy-done.3
  5.5 0.0 copy-start.4
  5.5 0.9 copy-done.4
  6.4 0.0 copy-start.5
  6.4 0.9 copy-done.5
  7.3 87.7 %outer_step.1 = (f32[4,8192]{1,0:T(4,128)S(1)}, f32[4,8192]{1,0:T(4,128)S(1)}, f32[4,2048]{1,0:T(4,128)S(1)}, f32[4,2048]{1,0:T(4,128)S(1)}, bf16[4,4,16,8192]{3,2,1,0:T(8,128)(2,1)S(1)}) custom-call(bf16[4,4,16,8192]{3,2,1,0:T(8,128)(2,1)S(1)} %bitcast.7, f32[4,8192]{1,0:T(4,128)S(1)} %bitcast.9, f32[4,8192]{1,0:T(4,128)S(1)} %bitcast.10, ...), custom_call_target="tpu_custom_call" | custom-call | tf_op jit(solution)/shard_map/outer_step/pallas_call | solution.py:407
  95.1 0.7 copy.16
  95.7 0.7 copy.17
  96.4 0.6 copy.18
  97.0 0.6 copy.19
  97.6 2.0 %copy.20 = bf16[256,8192]{1,0:T(8,128)(2,1)} copy(bf16[256,8192]{1,0:T(8,128)(2,1)S(1)} %bitcast.8) | data formatting | bytes 8388608
Async XLA Ops:
  0.6 2.2 %copy-start = (bf16[1,256,8192]{2,1,0:T(8,128)(2,1)S(1)}, bf16[1,256,8192]{2,1,0:T(8,128)(2,1)}, u32[]{:S(2)}) copy-start(bf16[1,256,8192]{2,1,0:T(8,128)(2,1)} %param.6) | copy-start | bytes 12582916
  2.8 0.9 copy-start.1
  3.7 0.9 copy-start.2
  4.6 0.9 copy-start.3
  5.5 0.9 copy-start.4
  6.4 0.9 copy-start.5

commit v2 on v1

--- a/solution.py
+++ b/solution.py
@@ -62,6 +62,25 @@
         return [self.own(self.i, 1), land.at[0, 1], land.at[1, 2]]
 
 
+class Direct(Ring):
+    def __init__(self, net, i, to, raw, land):
+        self.net, self.i, self.to, self.own, self.land = net, i, to, raw, land
+
+    def start(self):
+        self.b = [
+            self.net.send(self.own((self.i + d) % 4, hh), self.land.at[hh, d - 1], self.to[d - 1])
+            for d in (2, 1, 3)
+            for hh in range(2)
+        ]
+        self.c = []
+
+    def forward(self):
+        pass
+
+    def terms(self, hh):
+        return [self.own(self.i, hh)] + [self.land.at[hh, d] for d in range(3)]
+
+
 def add(dst, srcs):
     shape = dst.shape
     if len(shape) == 4:
@@ -107,10 +126,10 @@
 
 
 def kernel(
-    grad, m_ref, v_ref, p_ref, snap, mom,
+    grad, m_in, v_in, p_in, snap_in, mom_in,
     m_out, v_out, pn_out, mn_out, w_out,
-    G, LX1, LY1, AX1, AY1, SX1, SY1, L2, A2, M3, R3, Gs, PK, P1, P2, Pq, E, T, RT, Wb,
-    ss, rs, ls,
+    m_ref, v_ref, p_ref, snap, mom, G, LX1, LY1, AX1, AY1, SX1, SY1, L2, A2, M3, R3, Gs, PK, P1, P2, Pq, E, T, RT, Wb,
+    ss, rs, ls, bs,
 ):
     rep, f = lax.axis_index("rep"), lax.axis_index("fsdp")
     h, c = rep // 2, rep % 2
@@ -128,18 +147,30 @@
         cp.start()
         loc.append(cp)
 
-    peers = [dev(x=(x + a) % 4, y=(y + b) % 4) for a in range(4) for b in range(4) if a or b]
-    peers += [dev(z=(z + a) % 4, y=(y + b) % 4) for a in range(1, 4) for b in range(4)]
-    peers += [dev(h=1 - h, z=(z + a) % 4) for a in range(4)]
-    peers += [dev(h=hh, c=1 - c, z=zz) for hh in (h, 1 - h) for zz in (z, zp)]
-    bar = pltpu.get_barrier_semaphore()
-    for d in peers:
-        pl.semaphore_signal(bar, 1, device_id=d)
-    pl.semaphore_wait(bar, len(peers))
-
-    net = Net(ss, rs)
+    held = []
+    for n, (src, dst) in enumerate(
+        ((m_in, m_ref), (v_in, v_ref), (p_in, p_ref), (snap_in, snap), (mom_in, mom))
+    ):
+        cp = pltpu.make_async_copy(src, dst, ls.at[NR + n])
+        cp.start()
+        held.append(cp)
+
     xn, xp = dev(x=(x + 1) % 4), dev(x=(x + 3) % 4)
     yn, yp = dev(y=(y + 1) % 4), dev(y=(y + 3) % 4)
+    sib = dev(c=1 - c)
+    Zn, Zp = (Z + 1) % 8, (Z + 7) % 8
+    line = [dev(h=Zn // 4, z=Zn % 4), dev(h=Zp // 4, z=Zp % 4), sib]
+    bar = pltpu.get_barrier_semaphore()
+    for d in [xn, xp, yn, yp] + line:
+        pl.semaphore_signal(bar, 1, device_id=d)
+    pl.semaphore_wait(bar, 7)
+
+    def ahead(n):
+        for d in line:
+            pl.semaphore_signal(bs.at[n], 1, device_id=d)
+        pl.semaphore_wait(bs.at[n], 3)
+
+    net = Net(ss, rs)
 
     def first(r):
         k = r // 2
@@ -168,11 +199,17 @@
             def chunk(j, hh):
                 return SX1.at[k].at[pl.ds(2 * hh, 2), :, pl.ds(mo(j * CW), CW)]
 
+            if k == K - 1:
+                to = [dev(y=(y + d) % 4) for d in (1, 2, 3)]
+                return Direct(net, y, to, chunk, L2.at[r])
             return Ring(net, y, yn, yp, chunk, chunk, L2.at[r], A2.at[r])
 
         def chunk(j, hh):
             return SY1.at[k].at[pl.ds(2 * hh, 2), j]
 
+        if k == K - 1:
+            to = [dev(x=(x + d) % 4) for d in (1, 2, 3)]
+            return Direct(net, x, to, chunk, L2.at[r])
         return Ring(net, x, xn, xp, chunk, chunk, L2.at[r], A2.at[r])
 
     one = [first(r) for r in range(NR)]
@@ -215,23 +252,24 @@
     one[1].start()
     one[2].start()
     one[3].start()
+    for n in range(4):
+        ahead(n)
     for cp in loc:
         cp.wait()
     one[0].forward()
     one[1].forward()
-    finish_first(0)
     one[2].forward()
     one[3].forward()
+    finish_first(0)
+    finish_first(1)
     two[0].forward()
     two[1].forward()
     third = finish_second(0)
-    finish_first(1)
     two[2].forward()
     two[3].forward()
     third += finish_second(1)
     for cp in third:
         cp.wait_recv()
-
     for k in range(K):
         for dy in range(4):
             g = None
@@ -244,6 +282,8 @@
                     at = pl.ds(mo((2 * k + s) * W + ys * CW + t * HW), HW)
                     Gs[:, at] = rows4(g, 2 * s + t)
 
+    for cp in held:
+        cp.wait()
     top = None
     for q in range(4):
         parts = []
@@ -370,7 +410,6 @@
             right = net.send(large(p, i, hh), large(p, i, hh), nx)
             left = net.send(large(p, i, 1 - hh), large(p, i, 1 - hh), pv)
             near.append((p, hh, right, left))
-    sib = dev(c=1 - c)
     swaps = []
 
     def swap(p, i, hh):
@@ -400,11 +439,29 @@
         cp.wait_send()
 
 
+def flush(*refs):
+    n = len(refs) // 2
+    sems = refs[2 * n]
+    cps = [pltpu.make_async_copy(refs[i], refs[n + i], sems.at[i]) for i in range(n)]
+    for cp in cps:
+        cp.start()
+    for cp in cps:
+        cp.wait()
+
+
 def local(grad_parts, adam_m, adam_v, params_inner, snapshot, momentum):
     vmem = pl.BlockSpec(memory_space=pltpu.VMEM)
     hbm = pl.BlockSpec(memory_space=pl.ANY)
     V = pltpu.VMEM
-    m, v, pn, mn, w = pl.pallas_call(
+    args = (
+        grad_parts.reshape(4, 4, 16, D),
+        adam_m[0],
+        adam_v[0],
+        params_inner[0],
+        snapshot,
+        momentum,
+    )
+    outs = pl.pallas_call(
         kernel,
         out_shape=(
             jax.ShapeDtypeStruct((4, D), F32),
@@ -413,9 +470,14 @@
             jax.ShapeDtypeStruct((4, 2048), F32),
             jax.ShapeDtypeStruct((4, 4, 16, D), BF16),
         ),
-        in_specs=[hbm] + [vmem] * 5,
+        in_specs=[pl.BlockSpec(memory_space=pltpu.HBM)] * 6,
         out_specs=(vmem, vmem, vmem, vmem, hbm),
         scratch_shapes=[
+            V((4, D), F32),
+            V((4, D), F32),
+            V((4, D), F32),
+            V((4, D), F32),
+            V((4, D), F32),
             V((4, 4, 16, D), BF16),
             V((K, 2, 3, 2, 16, W), BF16),
             V((K, 2, 3, 2, 4, 16, CW), BF16),
@@ -438,20 +500,23 @@
             V((2, 16, 256), BF16),
             pltpu.SemaphoreType.DMA((NSEM,)),
             pltpu.SemaphoreType.DMA((NSEM,)),
-            pltpu.SemaphoreType.DMA((8,)),
+            pltpu.SemaphoreType.DMA((NR + 5,)),
+            pltpu.SemaphoreType.REGULAR((4,)),
         ],
         compiler_params=pltpu.CompilerParams(
             collective_id=0, has_side_effects=True, vmem_limit_bytes=40 * 2**20
         ),
         name="outer_step",
-    )(
-        grad_parts.reshape(4, 4, 16, D),
-        adam_m[0],
-        adam_v[0],
-        params_inner[0],
-        snapshot,
-        momentum,
-    )
+    )(*[pltpu.with_memory_space_constraint(a, pltpu.HBM) for a in args])
+    m, v, pn, mn, w = pl.pallas_call(
+        flush,
+        out_shape=tuple(jax.ShapeDtypeStruct(o.shape, o.dtype) for o in outs),
+        in_specs=[hbm] * 5,
+        out_specs=(hbm,) * 5,
+        scratch_shapes=[pltpu.SemaphoreType.DMA((5,))],
+        compiler_params=pltpu.CompilerParams(vmem_limit_bytes=2**20),
+        name="write_out",
+    )(*outs)
     return m[None], v[None], pn, mn, w.reshape(256, D)
 
 

time: 99.8 us -> 83.3 us (0.83)
  local copies, waits for them, and re-layouts: 11.3 us -> 0 us
  Pallas kernels: 87.7 us -> 82.6 us
    unnamed x17 -> x0, local copies, waits for them, and re-layouts: 11.3 us -> none
    pallas_call x1, Pallas kernels: 87.7 us -> 80.4 us  [local(): pl.pallas_call(kernel, out_shape=(jax.ShapeDtypeStruct((4, D), F32), jax....]
    pallas_call x0 -> x1, Pallas kernels: none -> 2.17 us  [local(): pl.pallas_call(flush, out_shape=tuple((jax.ShapeDtypeStruct(o.shape, o.dt...]
where the time goes in v2:
time: 83.3 us; the launch traced here: 83.2 us
  Pallas kernels  82.6 us (99%)
    pallas_call x1, Pallas kernels, local(): pl.pallas_call(kernel, out_shape=(jax.ShapeDtypeStruct((4, D), F32), jax....  80.4 us
    pallas_call x1, Pallas kernels, local(): pl.pallas_call(flush, out_shape=tuple((jax.ShapeDtypeStruct(o.shape, o.dt...  2.17 us

profile of v2, /device:TPU:1, one launch (start us, length us, event | category | flops | bytes accessed | tf_op | source)
XLA Modules:
  0.0 83.2 jit_solution(13738116249740464818)
XLA Ops:
  0.6 80.4 %outer_step.1 = (f32[4,8192]{1,0:T(4,128)S(1)}, f32[4,8192]{1,0:T(4,128)S(1)}, f32[4,2048]{1,0:T(4,128)S(1)}, f32[4,2048]{1,0:T(4,128)S(1)}, bf16[4,4,16,8192]{3,2,1,0:T(8,128)(2,1)S(1)}) custom-call(bf16[4,4,16,8192]{3,2,1,0:T(8,128)(2,1)} %bitcast.7, f32[4,8192]{1,0:T(4,128)} %bitcast.8, f32[4,8192]{1,0:T(4,128)} %bitcast.9, f32[4,8192]{1,0:T(4,128)} %bitcast.10, ...), custom_call_target="tpu_custom_call" | custom-call | tf_op jit(solution)/shard_map/outer_step/pallas_call | solution.py:464
  81.1 2.2 %write_out.1 = (f32[4,8192]{1,0:T(4,128)}, f32[4,8192]{1,0:T(4,128)}, f32[4,2048]{1,0:T(4,128)}, f32[4,2048]{1,0:T(4,128)}, bf16[4,4,16,8192]{3,2,1,0:T(8,128)(2,1)}) custom-call(f32[4,8192]{1,0:T(4,128)S(1)} %get-tuple-element.15.refs_0_, f32[4,8192]{1,0:T(4,128)S(1)} %get-tuple-element.16.refs_1_, f32[4,2048]{1,0:T(4,128)S(1)} %get-tuple-element.17.refs_2_, ...), custom_call_target="tpu_custom_call" | custom-call | tf_op jit(solution)/shard_map/write_out/pallas_call | solution.py:511

commit v3 on v2

--- a/solution.py
+++ b/solution.py
@@ -13,7 +13,7 @@
 W = D // NR
 CW = W // 4
 HW = CW // 2
-NSEM = 200
+NSEM = 240
 F32 = jnp.float32
 BF16 = jnp.bfloat16
 
@@ -29,12 +29,20 @@
         self.raw, self.own, self.land, self.acc = raw, own, land, acc
 
     def start(self):
+        self.start_far()
+        self.start_near()
+
+    def start_far(self):
         i, net = self.i, self.net
-        nxt, prv, far = (i + 1) % 4, (i + 3) % 4, (i + 2) % 4
+        far = (i + 2) % 4
         self.a = [
             net.send(self.raw(far, 0), self.land.at[0, 0], self.to_next),
             net.send(self.raw(far, 1), self.land.at[1, 0], self.to_prev),
         ]
+
+    def start_near(self):
+        i, net = self.i, self.net
+        nxt, prv = (i + 1) % 4, (i + 3) % 4
         self.b = [
             net.send(self.raw(nxt, 1), self.land.at[0, 1], self.to_next),
             net.send(self.raw(prv, 0), self.land.at[1, 1], self.to_prev),
@@ -121,6 +129,10 @@
         return cp
 
 
+def offsets(yy):
+    return [p * 1024 + yy * 256 + t * 128 for p in range(2) for t in range(2)]
+
+
 def rows4(v, b):
     return v[4 * b : 4 * b + 4]
 
@@ -128,7 +140,7 @@
 def kernel(
     grad, m_in, v_in, p_in, snap_in, mom_in,
     m_out, v_out, pn_out, mn_out, w_out,
-    m_ref, v_ref, p_ref, snap, mom, G, LX1, LY1, AX1, AY1, SX1, SY1, L2, A2, M3, R3, Gs, PK, P1, P2, Pq, E, T, RT, Wb,
+    m_ref, v_ref, p_ref, snap, mom, G, LX1, LY1, AX1, AY1, SX1, SY1, L2, A2, M3, R3, Gs, PK, P1, P2, Pq, E, X, SM, SX, Wb,
     ss, rs, ls, bs,
 ):
     rep, f = lax.axis_index("rep"), lax.axis_index("fsdp")
@@ -250,21 +262,32 @@
 
     one[0].start()
     one[1].start()
-    one[2].start()
-    one[3].start()
+    one[2].start_far()
+    one[3].start_far()
     for n in range(4):
         ahead(n)
     for cp in loc:
         cp.wait()
     one[0].forward()
     one[1].forward()
+    one[2].start_near()
+    one[3].start_near()
+    finish_first(0)
     one[2].forward()
     one[3].forward()
-    finish_first(0)
-    finish_first(1)
     two[0].forward()
     two[1].forward()
+    finish_first(1)
     third = finish_second(0)
+    for cp in held:
+        cp.wait()
+    for n, ref in enumerate((snap, mom)):
+        for yy in range(4):
+            SM[yy, n] = jnp.concatenate(
+                [ref[:, pl.ds(mo(rep * 2048 + o), 128)] for o in offsets(yy)], 0
+            )
+    sm = [net.send(SM.at[(y + d) % 4], SX.at[y], dev(y=(y + d) % 4)) for d in (2, 1, 3)]
+    SX[y] = SM[y]
     two[2].forward()
     two[3].forward()
     third += finish_second(1)
@@ -282,8 +305,6 @@
                     at = pl.ds(mo((2 * k + s) * W + ys * CW + t * HW), HW)
                     Gs[:, at] = rows4(g, 2 * s + t)
 
-    for cp in held:
-        cp.wait()
     top = None
     for q in range(4):
         parts = []
@@ -299,7 +320,9 @@
             parts.append(pseudo)
             size = jnp.abs(pseudo)
             top = size if top is None else jnp.maximum(top, size)
-        Pq[q] = jnp.concatenate(parts, 0).astype(BF16)
+        wide = jnp.concatenate(parts, 1)
+        for yy in range(4):
+            Pq[q, yy] = jnp.concatenate([wide[:, o : o + 128] for o in offsets(yy)], 0).astype(BF16)
     tile = functools.reduce(jnp.maximum, [top[:, 128 * i : 128 * i + 128] for i in range(4)])
     PK[0] = jnp.concatenate([tile, tile], 0)
 
@@ -314,9 +337,12 @@
         return (1 - h if dr // 2 else h), (1 - c if dr % 2 else c)
 
     sent_e = []
-    for dr in (3, 2, 1):
+    for dr in (3, 2, 1, 0):
         h2, c2 = flip(dr)
-        sent_e.append(net.send(Pq.at[2 * h2 + c2], E.at[dr], dev(h=h2, c=c2)))
+        for d in (2, 1, 3, 0):
+            if dr or d:
+                to = (y + d) % 4
+                sent_e.append(net.send(Pq.at[2 * h2 + c2, to], X.at[dr, y], dev(h=h2, c=c2, y=to)))
     peak = PK[0]
     for cp in got:
         cp.wait_recv()
@@ -331,44 +357,25 @@
                 got.append(
                     net.send(PK.at[1], P2.at[e, dr], dev(h=h2, c=c2, z=zp if e else z))
                 )
-    for cp in got + sent_e:
-        cp.wait_recv()
-    total = None
+    for cp in sm + sent_e:
+        cp.wait_recv()
+    for cp in got:
+        cp.wait_recv()
+    factors = []
     for dr in range(4):
         high = jnp.maximum(P2[0, dr] if dr else peak, P2[1, dr])
         high = jnp.max(high, axis=(0, 1), keepdims=True)
-        factor = 0.5 / jnp.maximum(high, 0.5)
-        term = (E[dr] if dr else Pq[rep]).astype(F32) * factor
-        total = term if total is None else total + term
-    averaged = total / 4
+        factors.append(0.5 / jnp.maximum(high, 0.5))
+    X[0, y] = Pq[rep, y]
     new = []
-    for t in range(4):
-        avg = rows4(averaged, t)
-        at = pl.ds(mo(rep * 2048 + t * 512), 512)
-        m_new = 0.9 * mom[:, at] + avg
-        p_new = snap[:, at] - 0.7 * (avg + 0.9 * m_new)
-        mn_out[:, pl.ds(t * 512, 512)] = m_new
-        pn_out[:, pl.ds(t * 512, 512)] = p_new
-        new.append(p_new)
-    new = jnp.concatenate(new, 1)
-    for yy in range(4):
-        pieces = [
-            new[:, p * 1024 + yy * 256 + t * 128 : p * 1024 + yy * 256 + t * 128 + 128]
-            for p in range(2)
-            for t in range(2)
-        ]
-        T[yy] = jnp.concatenate(pieces, 0).astype(BF16)
-    got = [
-        net.send(T.at[(y + d) % 4], RT.at[y], dev(y=(y + d) % 4)) for d in (2, 1, 3)
-    ]
-    RT[y] = T[y]
-    for cp in got:
-        cp.wait_recv()
+    for ys in range(4):
+        terms = [X[dr, ys].astype(F32) * factors[dr] for dr in range(4)]
+        avg = functools.reduce(jnp.add, terms) / 4
+        new.append(SX[ys, 0] - 0.7 * (avg + 0.9 * (0.9 * SX[ys, 1] + avg)))
     for p in range(2):
         for t in range(2):
-            b = 2 * p + t
             Wb[p, :, pl.ds(t * 128, 128)] = jnp.concatenate(
-                [rows4(RT[ys].astype(F32), b) for ys in range(4)], 0
+                [rows4(v, 2 * p + t) for v in new], 0
             ).astype(BF16)
 
     def small(p):
@@ -378,61 +385,111 @@
         cp = pltpu.make_async_copy(Wb.at[p], small(p), ls.at[p])
         cp.start()
         loc[p] = cp
-    got = []
-    for d in (4, 3, 5, 2, 6, 1, 7):
-        Z2 = (Z + d) % 8
-        for p in range(2):
-            got.append(net.send(Wb.at[p], small(p), dev(h=Z2 // 4, z=Z2 % 4)))
+    strips = [[], []]
+    for s in range(2):
+        for d in (2, 1, 3, 0):
+            if s or d:
+                for p in range(2):
+                    to = dev(h=1 - h if s else h, z=(z + d) % 4)
+                    strips[s].append(net.send(Wb.at[p], small(p), to))
+
+    wide_e = []
+    for dr in (3, 2, 1):
+        h2, c2 = flip(dr)
+        wide_e.append(net.send(Pq.at[2 * h2 + c2], E.at[dr], dev(h=h2, c=c2)))
+
+    def part(p, s, mid, last):
+        q = 2 * (1 - h if s else h) + c
+        if p == 0:
+            return w_out.at[:, last, :, pl.ds(mo(q * 2048 + mid * 256), 256)]
+        return w_out.at[:, mid, :, pl.ds(mo(q * 2048 + 1024 + last * 256), 256)]
+
+    def large(p, s, last):
+        q = 2 * (1 - h if s else h) + c
+        if p == 0:
+            return w_out.at[:, last, :, pl.ds(mo(q * 2048), 1024)]
+        return w_out.at[:, :, :, pl.ds(mo(q * 2048 + 1024 + last * 256), 256)]
+
+    ways = ((y, x, xn, xp), (x, y, yn, yp))
+    mids, near, far, swaps = {}, {}, [], []
+
+    def send_mid(s):
+        for d in (2, 1, 3):
+            for p, (m, la, _, _) in enumerate(ways):
+                to = dev(y=(y + d) % 4) if p == 0 else dev(x=(x + d) % 4)
+                mids[p, s, d] = net.send(part(p, s, m, la), part(p, s, m, la), to)
+
+    def send_last(s, d):
+        for p, (m, la, nx, pv) in enumerate(ways):
+            if d:
+                mids[p, s, d].wait_recv()
+            blk = part(p, s, (m + 4 - d) % 4, la)
+            near[p, s, d] = net.send(blk, blk, nx), net.send(blk, blk, pv)
+
+    def pass_on(s, d):
+        for p, (m, la, nx, pv) in enumerate(ways):
+            mid = (m + 4 - d) % 4
+            from_prev, from_next = near[p, s, d]
+            if d % 2 == 0:
+                from_prev.wait_recv()
+                blk = part(p, s, mid, (la + 3) % 4)
+                far.append(net.send(blk, blk, nx))
+                from_next.wait_recv()
+            else:
+                from_next.wait_recv()
+                blk = part(p, s, mid, (la + 1) % 4)
+                far.append(net.send(blk, blk, pv))
+                from_prev.wait_recv()
+
+    def swap(s, d):
+        for p, (m, la, nx, pv) in enumerate(ways):
+            blk = large(p, s, (la + 4 - d) % 4)
+            swaps.append(net.send(blk, blk, sib))
+
     for p in range(2):
         loc[p].wait()
-    for cp in got:
-        cp.wait_recv()
-    got = []
-    for d in (2, 1, 3):
-        for p, to in ((0, dev(y=(y + d) % 4)), (1, dev(x=(x + d) % 4))):
-            for hh in range(2):
-                blk = w_out.at[
-                    :, x, :, pl.ds(mo((2 * hh + c) * 2048 + p * 1024 + y * 256), 256)
-                ]
-                got.append(net.send(blk, blk, to))
-    for cp in got:
-        cp.wait_recv()
-
-    def large(p, i, hh):
-        if p == 0:
-            return w_out.at[:, i, :, pl.ds(mo((2 * hh + c) * 2048), 1024)]
-        return w_out.at[:, :, :, pl.ds(mo((2 * hh + c) * 2048 + 1024 + i * 256), 256)]
-
-    ways = ((x, xn, xp), (y, yn, yp))
-    near = []
-    for hh in range(2):
-        for p, (i, nx, pv) in enumerate(ways):
-            right = net.send(large(p, i, hh), large(p, i, hh), nx)
-            left = net.send(large(p, i, 1 - hh), large(p, i, 1 - hh), pv)
-            near.append((p, hh, right, left))
-    swaps = []
-
-    def swap(p, i, hh):
-        swaps.append(net.send(large(p, i, hh), large(p, i, hh), sib))
-
-    for p, (i, _, _) in enumerate(ways):
-        for hh in range(2):
-            swap(p, i, hh)
-    far = []
-    for p, hh, right, left in near:
-        i, nx, pv = ways[p]
-        right.wait_recv()
-        prv, nxt = (i + 3) % 4, (i + 1) % 4
-        if hh == 0:
-            far.append((p, 0, net.send(large(p, prv, 0), large(p, prv, 0), nx)))
-        swap(p, prv, hh)
-        left.wait_recv()
-        if hh == 0:
-            far.append((p, 1, net.send(large(p, nxt, 1), large(p, nxt, 1), pv)))
-        swap(p, nxt, 1 - hh)
-    for p, hh, cp in far:
-        cp.wait_recv()
-        swap(p, (ways[p][0] + 2) % 4, hh)
+    for s in range(2):
+        for cp in strips[s]:
+            cp.wait_recv()
+        send_mid(s)
+        send_last(s, 0)
+
+    order = (1, 3, 2)
+    for d in order:
+        send_last(0, d)
+    swap(0, 0)
+    pass_on(0, 0)
+    for d in order:
+        send_last(1, d)
+    swap(1, 0)
+    for cp in wide_e:
+        cp.wait_recv()
+    for yy in range(4):
+        terms = [
+            (E[dr, yy] if dr else Pq[rep, yy]).astype(F32) * factors[dr] for dr in range(4)
+        ]
+        averaged = functools.reduce(jnp.add, terms) / 4
+        m_new = 0.9 * SM[yy, 1] + averaged
+        p_new = SM[yy, 0] - 0.7 * (averaged + 0.9 * m_new)
+        for b, o in enumerate(offsets(yy)):
+            mn_out[:, o : o + 128] = rows4(m_new, b)
+            pn_out[:, o : o + 128] = rows4(p_new, b)
+
+    for d in order:
+        pass_on(0, d)
+    swap(0, 1)
+    swap(0, 3)
+    pass_on(1, 0)
+    for d in order:
+        pass_on(1, d)
+    swap(1, 1)
+    swap(1, 3)
+    for cp in far[:8]:
+        cp.wait_recv()
+    swap(0, 2)
+    for cp in far[8:]:
+        cp.wait_recv()
+    swap(1, 2)
     for cp in swaps:
         cp.wait_recv()
     for cp in net.sent:
@@ -493,10 +550,11 @@
             V((2, 8, 128), F32),
             V((16, 8, 128), F32),
             V((2, 4, 8, 128), F32),
-            V((4, 16, 512), BF16),
-            V((4, 16, 512), BF16),
-            V((4, 16, 128), BF16),
-            V((4, 16, 128), BF16),
+            V((4, 4, 16, 128), BF16),
+            V((4, 4, 16, 128), BF16),
+            V((4, 4, 16, 128), BF16),
+            V((4, 2, 16, 128), F32),
+            V((4, 2, 16, 128), F32),
             V((2, 16, 256), BF16),
             pltpu.SemaphoreType.DMA((NSEM,)),
             pltpu.SemaphoreType.DMA((NSEM,)),

time: 83.3 us -> 80.2 us (0.963)
  Pallas kernels: 82.6 us -> 79.5 us
    pallas_call x1, Pallas kernels: 80.4 us -> 77.4 us  [local(): pl.pallas_call(kernel, out_shape=(jax.ShapeDtypeStruct((4, D), F32), jax....]
where the time goes in v3:
time: 80.2 us
  Pallas kernels  79.5 us (99%)
    pallas_call x1, Pallas kernels, local(): pl.pallas_call(kernel, out_shape=(jax.ShapeDtypeStruct((4, D), F32), jax....  77.4 us
    pallas_call x1, Pallas kernels, local(): pl.pallas_call(flush, out_shape=tuple((jax.ShapeDtypeStruct(o.shape, o.dt...  2.17 us

profile of v3, /device:TPU:1, one launch (start us, length us, event | category | flops | bytes accessed | tf_op | source)
XLA Modules:
  0.0 80.2 jit_solution(14146871718749742084)
XLA Ops:
  0.6 77.4 %outer_step.1 = (f32[4,8192]{1,0:T(4,128)S(1)}, f32[4,8192]{1,0:T(4,128)S(1)}, f32[4,2048]{1,0:T(4,128)S(1)}, f32[4,2048]{1,0:T(4,128)S(1)}, bf16[4,4,16,8192]{3,2,1,0:T(8,128)(2,1)S(1)}) custom-call(bf16[4,4,16,8192]{3,2,1,0:T(8,128)(2,1)} %bitcast.7, f32[4,8192]{1,0:T(4,128)} %bitcast.8, f32[4,8192]{1,0:T(4,128)} %bitcast.9, f32[4,8192]{1,0:T(4,128)} %bitcast.10, ...), custom_call_target="tpu_custom_call" | custom-call | tf_op jit(solution)/shard_map/outer_step/pallas_call | solution.py:521
  78.0 2.2 %write_out.1 = (f32[4,8192]{1,0:T(4,128)}, f32[4,8192]{1,0:T(4,128)}, f32[4,2048]{1,0:T(4,128)}, f32[4,2048]{1,0:T(4,128)}, bf16[4,4,16,8192]{3,2,1,0:T(8,128)(2,1)}) custom-call(f32[4,8192]{1,0:T(4,128)S(1)} %get-tuple-element.15.refs_0_, f32[4,8192]{1,0:T(4,128)S(1)} %get-tuple-element.16.refs_1_, f32[4,2048]{1,0:T(4,128)S(1)} %get-tuple-element.17.refs_2_, ...), custom_call_target="tpu_custom_call" | custom-call | tf_op jit(solution)/shard_map/write_out/pallas_call | solution.py:569

commit v4 on v3

--- a/solution.py
+++ b/solution.py
@@ -9,11 +9,13 @@
 
 D = 8192
 K = 2
+PIECE = (256, 128)
 NR = 2 * K
-W = D // NR
-CW = W // 4
-HW = CW // 2
-NSEM = 240
+WS = (2048, 1536)
+CWS = tuple(w // 4 for w in WS)
+ZO = 2 * sum(WS)
+ZW = D - ZO
+NSEM = 260
 F32 = jnp.float32
 BF16 = jnp.bfloat16
 
@@ -39,6 +41,11 @@
             net.send(self.raw(far, 0), self.land.at[0, 0], self.to_next),
             net.send(self.raw(far, 1), self.land.at[1, 0], self.to_prev),
         ]
+
+    def leave(self, copies):
+        for cp in copies:
+            cp.wait_send()
+            self.net.sent = [other for other in self.net.sent if other is not cp]
 
     def start_near(self):
         i, net = self.i, self.net
@@ -103,13 +110,14 @@
     else:
 
         def body(j, _):
-            at = pl.ds(mo(j * 512, 512), 512)
+            at = pl.ds(mo(j * step, step), step)
             dst[:, :, at] = functools.reduce(
                 jnp.add, [s[:, :, at].astype(F32) for s in srcs]
             ).astype(BF16)
             return 0
 
-        lax.fori_loop(0, shape[2] // 512, body, 0)
+        step = 512 if shape[2] % 512 == 0 else shape[2]
+        lax.fori_loop(0, shape[2] // step, body, 0)
 
 
 class Net:
@@ -140,7 +148,7 @@
 def kernel(
     grad, m_in, v_in, p_in, snap_in, mom_in,
     m_out, v_out, pn_out, mn_out, w_out,
-    m_ref, v_ref, p_ref, snap, mom, G, LX1, LY1, AX1, AY1, SX1, SY1, L2, A2, M3, R3, Gs, PK, P1, P2, Pq, E, X, SM, SX, Wb,
+    m_ref, v_ref, p_ref, snap, mom, G, LX1, LY1, AX1, AY1, SX1, SY1, L2, A2, M3, R3, LC1, SC, LC2, MC, RC, Gs, PK, P1, P2, Pq, E, X, SM, SX, Wb,
     ss, rs, ls, bs,
 ):
     rep, f = lax.axis_index("rep"), lax.axis_index("fsdp")
@@ -154,7 +162,7 @@
 
     loc = []
     for r in range(NR):
-        at = pl.ds(r * W, W)
+        at = pl.ds(r * 2048, 2048)
         cp = pltpu.make_async_copy(grad.at[:, :, :, at], G.at[:, :, :, at], ls.at[r])
         cp.start()
         loc.append(cp)
@@ -184,24 +192,28 @@
 
     net = Net(ss, rs)
 
+    def origin(k, s):
+        return 2 * sum(WS[:k]) + s * WS[k]
+
     def first(r):
         k = r // 2
+        o, w, cw = origin(k, r % 2), WS[k], CWS[k]
         if r % 2 == 0:
 
             def chunk(src, j, hh):
-                return src.at[pl.ds(2 * hh, 2), j, :, pl.ds(r * W, W)]
+                return src.at[pl.ds(2 * hh, 2), j, :, pl.ds(o, w)]
 
             return Ring(
                 net, x, xn, xp, functools.partial(chunk, grad), functools.partial(chunk, G),
-                LX1.at[k], AX1.at[k],
+                LX1[k], AX1[k],
             )
 
         def chunk(src, j, hh):
-            return src.at[pl.ds(2 * hh, 2), :, :, pl.ds(mo(r * W + j * CW), CW)]
+            return src.at[pl.ds(2 * hh, 2), :, :, pl.ds(mo(o + j * cw), cw)]
 
         return Ring(
             net, y, yn, yp, functools.partial(chunk, grad), functools.partial(chunk, G),
-            LY1.at[k], AY1.at[k],
+            LY1[k], AY1[k],
         )
 
     def second(r):
@@ -209,20 +221,20 @@
         if r % 2 == 0:
 
             def chunk(j, hh):
-                return SX1.at[k].at[pl.ds(2 * hh, 2), :, pl.ds(mo(j * CW), CW)]
+                return SX1[k].at[pl.ds(2 * hh, 2), :, pl.ds(mo(j * CWS[k]), CWS[k])]
 
             if k == K - 1:
                 to = [dev(y=(y + d) % 4) for d in (1, 2, 3)]
-                return Direct(net, y, to, chunk, L2.at[r])
-            return Ring(net, y, yn, yp, chunk, chunk, L2.at[r], A2.at[r])
+                return Direct(net, y, to, chunk, L2[k].at[r % 2])
+            return Ring(net, y, yn, yp, chunk, chunk, L2[k].at[r % 2], A2[k].at[r % 2])
 
         def chunk(j, hh):
-            return SY1.at[k].at[pl.ds(2 * hh, 2), j]
+            return SY1[k].at[pl.ds(2 * hh, 2), j]
 
         if k == K - 1:
             to = [dev(x=(x + d) % 4) for d in (1, 2, 3)]
-            return Direct(net, x, to, chunk, L2.at[r])
-        return Ring(net, x, xn, xp, chunk, chunk, L2.at[r], A2.at[r])
+            return Direct(net, x, to, chunk, L2[k].at[r % 2])
+        return Ring(net, x, xn, xp, chunk, chunk, L2[k].at[r % 2], A2[k].at[r % 2])
 
     one = [first(r) for r in range(NR)]
     two = [second(r) for r in range(NR)]
@@ -230,7 +242,7 @@
     def finish_first(k):
         for r in (2 * k, 2 * k + 1):
             one[r].wait()
-            dst = (SX1 if r % 2 == 0 else SY1).at[k]
+            dst = (SX1 if r % 2 == 0 else SY1)[k]
             for hh in range(2):
                 add(dst.at[pl.ds(2 * hh, 2)], one[r].terms(hh))
         for r in (2 * k, 2 * k + 1):
@@ -241,18 +253,21 @@
         for ring in rings:
             ring.wait()
         for zz in range(4):
-            halves = []
+            pieces = []
             for ring in rings:
                 s = functools.reduce(
                     jnp.add, [t[zz % 2].astype(F32) for t in ring.terms(zz // 2)]
                 )
-                halves += [s[:, :HW], s[:, HW:]]
+                pw = PIECE[k]
+                pieces += [s[:, o : o + pw] for o in range(0, CWS[k], pw)]
+            while len(pieces) % 4:
+                pieces.append(jnp.zeros_like(pieces[0]))
             for yy in range(4):
-                M3[k, zz, yy] = jnp.concatenate([rows4(s, yy) for s in halves], 0).astype(BF16)
+                M3[k][zz, yy] = jnp.concatenate([rows4(s, yy) for s in pieces], 0).astype(BF16)
         return [
             net.send(
-                M3.at[k, (z + dz) % 4, (y + dy) % 4],
-                R3.at[k, dz, dy],
+                M3[k].at[(z + dz) % 4, (y + dy) % 4],
+                R3[k].at[dz, dy],
                 dev(z=(z + dz) % 4, y=(y + dy) % 4),
             )
             for dz in (2, 1, 3, 0)
@@ -260,16 +275,27 @@
             if dz or dy
         ]
 
-    one[0].start()
-    one[1].start()
+    one[0].start_far()
+    one[1].start_far()
+    ahead(0)
+    ahead(1)
+    one[0].leave(one[0].a + one[1].a)
+    one[0].start_near()
+    one[1].start_near()
     one[2].start_far()
     one[3].start_far()
-    for n in range(4):
-        ahead(n)
+    ahead(2)
+    ahead(3)
+    zcols = pl.ds(ZO, ZW)
+    zfirst = [
+        net.send(grad.at[(z + d) % 4, :, :, zcols], LC1.at[d - 1], dev(z=(z + d) % 4))
+        for d in (2, 1, 3)
+    ]
     for cp in loc:
         cp.wait()
     one[0].forward()
     one[1].forward()
+    one[0].leave(one[0].c + one[1].c)
     one[2].start_near()
     one[3].start_near()
     finish_first(0)
@@ -278,6 +304,12 @@
     two[0].forward()
     two[1].forward()
     finish_first(1)
+    for cp in zfirst:
+        cp.wait_recv()
+    add(SC, [G.at[z, :, :, zcols]] + [LC1.at[d] for d in range(3)])
+    zsecond = [
+        net.send(SC.at[(x + d) % 4], LC2.at[d - 1], dev(x=(x + d) % 4)) for d in (2, 1, 3)
+    ]
     third = finish_second(0)
     for cp in held:
         cp.wait()
@@ -291,19 +323,38 @@
     two[2].forward()
     two[3].forward()
     third += finish_second(1)
+    for cp in zsecond:
+        cp.wait_recv()
+    s = SC[x].astype(F32)
+    for d in range(3):
+        s = s + LC2[d].astype(F32)
+    for yy in range(4):
+        MC[yy] = jnp.concatenate(
+            [rows4(s[:, t * ZW // 4 : (t + 1) * ZW // 4], yy) for t in range(4)], 0
+        ).astype(BF16)
+    third += [
+        net.send(MC.at[(y + d) % 4], RC.at[d - 1], dev(y=(y + d) % 4)) for d in (2, 1, 3)
+    ]
     for cp in third:
         cp.wait_recv()
     for k in range(K):
         for dy in range(4):
             g = None
             for dz in range(4):
-                t = (R3[k, dz, dy] if dz or dy else M3[k, z, y]).astype(F32)
+                t = (R3[k][dz, dy] if dz or dy else M3[k][z, y]).astype(F32)
                 g = t if g is None else g + t
             ys = (y + 4 - dy) % 4
+            pw = PIECE[k]
+            n = CWS[k] // pw
             for s in range(2):
-                for t in range(2):
-                    at = pl.ds(mo((2 * k + s) * W + ys * CW + t * HW), HW)
-                    Gs[:, at] = rows4(g, 2 * s + t)
+                for t in range(n):
+                    at = pl.ds(mo(origin(k, s) + ys * CWS[k] + t * pw), pw)
+                    Gs[:, at] = rows4(g, n * s + t)
+    g = MC[y].astype(F32)
+    for d in range(3):
+        g = g + RC[d].astype(F32)
+    for t in range(4):
+        Gs[:, ZO + t * ZW // 4 : ZO + (t + 1) * ZW // 4] = rows4(g, t)
 
     top = None
     for q in range(4):
@@ -536,16 +587,21 @@
             V((4, D), F32),
             V((4, D), F32),
             V((4, 4, 16, D), BF16),
-            V((K, 2, 3, 2, 16, W), BF16),
-            V((K, 2, 3, 2, 4, 16, CW), BF16),
-            V((K, 2, 2, 16, W), BF16),
-            V((K, 2, 2, 4, 16, CW), BF16),
-            V((K, 4, 16, W), BF16),
-            V((K, 4, 4, 16, CW), BF16),
-            V((NR, 2, 3, 2, 16, CW), BF16),
-            V((NR, 2, 2, 16, CW), BF16),
-            V((K, 4, 4, 16, HW), BF16),
-            V((K, 4, 4, 16, HW), BF16),
+            [V((2, 3, 2, 16, w), BF16) for w in WS],
+            [V((2, 3, 2, 4, 16, w), BF16) for w in CWS],
+            [V((2, 2, 16, w), BF16) for w in WS],
+            [V((2, 2, 4, 16, w), BF16) for w in CWS],
+            [V((4, 16, w), BF16) for w in WS],
+            [V((4, 4, 16, w), BF16) for w in CWS],
+            [V((2, 2, 3, 2, 16, w), BF16) for w in CWS],
+            [V((2, 2, 2, 16, w), BF16) for w in CWS],
+            [V((4, 4, 16, 256), BF16), V((4, 4, 32, 128), BF16)],
+            [V((4, 4, 16, 256), BF16), V((4, 4, 32, 128), BF16)],
+            V((3, 4, 16, ZW), BF16),
+            V((4, 16, ZW), BF16),
+            V((3, 16, ZW), BF16),
+            V((4, 16, ZW // 4), BF16),
+            V((3, 16, ZW // 4), BF16),
             V((4, D), F32),
             V((2, 8, 128), F32),
             V((16, 8, 128), F32),

time: 80.2 us -> 78 us (0.973)
  Pallas kernels: 79.5 us -> 77.3 us
    pallas_call x1, Pallas kernels: 77.4 us -> 75.1 us  [local(): pl.pallas_call(kernel, out_shape=(jax.ShapeDtypeStruct((4, D), F32), jax....]
where the time goes in v4:
time: 78 us; the launch traced here: 77.9 us
  Pallas kernels  77.3 us (99%)
    pallas_call x1, Pallas kernels, local(): pl.pallas_call(kernel, out_shape=(jax.ShapeDtypeStruct((4, D), F32), jax....  75.1 us
    pallas_call x1, Pallas kernels, local(): pl.pallas_call(flush, out_shape=tuple((jax.ShapeDtypeStruct(o.shape, o.dt...  2.17 us

profile of v4, /device:TPU:1, one launch (start us, length us, event | category | flops | bytes accessed | tf_op | source)
XLA Modules:
  0.0 77.9 jit_solution(17596233397107065772)
XLA Ops:
  0.6 75.1 %outer_step.1 = (f32[4,8192]{1,0:T(4,128)S(1)}, f32[4,8192]{1,0:T(4,128)S(1)}, f32[4,2048]{1,0:T(4,128)S(1)}, f32[4,2048]{1,0:T(4,128)S(1)}, bf16[4,4,16,8192]{3,2,1,0:T(8,128)(2,1)S(1)}) custom-call(bf16[4,4,16,8192]{3,2,1,0:T(8,128)(2,1)} %bitcast.7, f32[4,8192]{1,0:T(4,128)} %bitcast.8, f32[4,8192]{1,0:T(4,128)} %bitcast.9, f32[4,8192]{1,0:T(4,128)} %bitcast.10, ...), custom_call_target="tpu_custom_call" | custom-call | tf_op jit(solution)/shard_map/outer_step/pallas_call | solution.py:572
  75.8 2.2 %write_out.1 = (f32[4,8192]{1,0:T(4,128)}, f32[4,8192]{1,0:T(4,128)}, f32[4,2048]{1,0:T(4,128)}, f32[4,2048]{1,0:T(4,128)}, bf16[4,4,16,8192]{3,2,1,0:T(8,128)(2,1)}) custom-call(f32[4,8192]{1,0:T(4,128)S(1)} %get-tuple-element.15.refs_0_, f32[4,8192]{1,0:T(4,128)S(1)} %get-tuple-element.16.refs_1_, f32[4,2048]{1,0:T(4,128)S(1)} %get-tuple-element.17.refs_2_, ...), custom_call_target="tpu_custom_call" | custom-call | tf_op jit(solution)/shard_map/write_out/pallas_call | solution.py:625

commit v5 on v4

--- a/solution.py
+++ b/solution.py
@@ -310,7 +310,7 @@
     zsecond = [
         net.send(SC.at[(x + d) % 4], LC2.at[d - 1], dev(x=(x + d) % 4)) for d in (2, 1, 3)
     ]
-    third = finish_second(0)
+    early = finish_second(0)
     for cp in held:
         cp.wait()
     for n, ref in enumerate((snap, mom)):
@@ -322,7 +322,7 @@
     SX[y] = SM[y]
     two[2].forward()
     two[3].forward()
-    third += finish_second(1)
+    third = finish_second(1)
     for cp in zsecond:
         cp.wait_recv()
     s = SC[x].astype(F32)
@@ -335,9 +335,8 @@
     third += [
         net.send(MC.at[(y + d) % 4], RC.at[d - 1], dev(y=(y + d) % 4)) for d in (2, 1, 3)
     ]
-    for cp in third:
-        cp.wait_recv()
-    for k in range(K):
+
+    def collect(k):
         for dy in range(4):
             g = None
             for dz in range(4):
@@ -350,14 +349,7 @@
                 for t in range(n):
                     at = pl.ds(mo(origin(k, s) + ys * CWS[k] + t * pw), pw)
                     Gs[:, at] = rows4(g, n * s + t)
-    g = MC[y].astype(F32)
-    for d in range(3):
-        g = g + RC[d].astype(F32)
-    for t in range(4):
-        Gs[:, ZO + t * ZW // 4 : ZO + (t + 1) * ZW // 4] = rows4(g, t)
-
-    top = None
-    for q in range(4):
+    def adam(q, top):
         parts = []
         for t in range(4):
             at = pl.ds(q * 2048 + t * 512, 512)
@@ -374,13 +366,28 @@
         wide = jnp.concatenate(parts, 1)
         for yy in range(4):
             Pq[q, yy] = jnp.concatenate([wide[:, o : o + 128] for o in offsets(yy)], 0).astype(BF16)
+        return top
+
+    for cp in early:
+        cp.wait_recv()
+    collect(0)
+    top = adam(1, adam(0, None))
+    for cp in third:
+        cp.wait_recv()
+    collect(1)
+    g = MC[y].astype(F32)
+    for d in range(3):
+        g = g + RC[d].astype(F32)
+    for t in range(4):
+        Gs[:, ZO + t * ZW // 4 : ZO + (t + 1) * ZW // 4] = rows4(g, t)
+    top = adam(3, adam(2, top))
     tile = functools.reduce(jnp.maximum, [top[:, 128 * i : 128 * i + 128] for i in range(4)])
     PK[0] = jnp.concatenate([tile, tile], 0)
 
     got = [
         net.send(PK.at[0], P1.at[4 * a + b], dev(x=(x + a) % 4, y=(y + b) % 4))
-        for a in range(4)
-        for b in range(4)
+        for a in (2, 1, 3, 0)
+        for b in (2, 1, 3, 0)
         if a or b
     ]
 

time: 78 us -> 77.5 us (level)
  no operation moved by 1% of the time
where the time goes in v5:
time: 77.5 us; the launch traced here: 77.4 us
  Pallas kernels  76.7 us (99%)
    pallas_call x1, Pallas kernels, local(): pl.pallas_call(kernel, out_shape=(jax.ShapeDtypeStruct((4, D), F32), jax....  74.6 us
    pallas_call x1, Pallas kernels, local(): pl.pallas_call(flush, out_shape=tuple((jax.ShapeDtypeStruct(o.shape, o.dt...  2.17 us

profile of v5, /device:TPU:1, one launch (start us, length us, event | category | flops | bytes accessed | tf_op | source)
XLA Modules:
  0.0 77.4 jit_solution(302319415392228866)
XLA Ops:
  0.6 74.6 %outer_step.1 = (f32[4,8192]{1,0:T(4,128)S(1)}, f32[4,8192]{1,0:T(4,128)S(1)}, f32[4,2048]{1,0:T(4,128)S(1)}, f32[4,2048]{1,0:T(4,128)S(1)}, bf16[4,4,16,8192]{3,2,1,0:T(8,128)(2,1)S(1)}) custom-call(bf16[4,4,16,8192]{3,2,1,0:T(8,128)(2,1)} %bitcast.7, f32[4,8192]{1,0:T(4,128)} %bitcast.8, f32[4,8192]{1,0:T(4,128)} %bitcast.9, f32[4,8192]{1,0:T(4,128)} %bitcast.10, ...), custom_call_target="tpu_custom_call" | custom-call | tf_op jit(solution)/shard_map/outer_step/pallas_call | solution.py:579
  75.2 2.2 %write_out.1 = (f32[4,8192]{1,0:T(4,128)}, f32[4,8192]{1,0:T(4,128)}, f32[4,2048]{1,0:T(4,128)}, f32[4,2048]{1,0:T(4,128)}, bf16[4,4,16,8192]{3,2,1,0:T(8,128)(2,1)}) custom-call(f32[4,8192]{1,0:T(4,128)S(1)} %get-tuple-element.15.refs_0_, f32[4,8192]{1,0:T(4,128)S(1)} %get-tuple-element.16.refs_1_, f32[4,2048]{1,0:T(4,128)S(1)} %get-tuple-element.17.refs_2_, ...), custom_call_target="tpu_custom_call" | custom-call | tf_op jit(solution)/shard_map/write_out/pallas_call | solution.py:632

commit v6 on v5

--- a/solution.py
+++ b/solution.py
@@ -271,7 +271,7 @@
                 dev(z=(z + dz) % 4, y=(y + dy) % 4),
             )
             for dz in (2, 1, 3, 0)
-            for dy in range(4)
+            for dy in (2, 1, 3, 0)
             if dz or dy
         ]
 

time: 77.5 us -> 77.9 us (level)
  no operation moved by 1% of the time
where the time goes in v6:
time: 77.9 us; the launch traced here: 77.8 us
  Pallas kernels  77.2 us (99%)
    pallas_call x1, Pallas kernels, local(): pl.pallas_call(kernel, out_shape=(jax.ShapeDtypeStruct((4, D), F32), jax....  75 us
    pallas_call x1, Pallas kernels, local(): pl.pallas_call(flush, out_shape=tuple((jax.ShapeDtypeStruct(o.shape, o.dt...  2.17 us

profile of v6, /device:TPU:1, one launch (start us, length us, event | category | flops | bytes accessed | tf_op | source)
XLA Modules:
  0.0 77.8 jit_solution(4019794710063355221)
XLA Ops:
  0.6 75.0 %outer_step.1 = (f32[4,8192]{1,0:T(4,128)S(1)}, f32[4,8192]{1,0:T(4,128)S(1)}, f32[4,2048]{1,0:T(4,128)S(1)}, f32[4,2048]{1,0:T(4,128)S(1)}, bf16[4,4,16,8192]{3,2,1,0:T(8,128)(2,1)S(1)}) custom-call(bf16[4,4,16,8192]{3,2,1,0:T(8,128)(2,1)} %bitcast.7, f32[4,8192]{1,0:T(4,128)} %bitcast.8, f32[4,8192]{1,0:T(4,128)} %bitcast.9, f32[4,8192]{1,0:T(4,128)} %bitcast.10, ...), custom_call_target="tpu_custom_call" | custom-call | tf_op jit(solution)/shard_map/outer_step/pallas_call | solution.py:579
  75.6 2.2 %write_out.1 = (f32[4,8192]{1,0:T(4,128)}, f32[4,8192]{1,0:T(4,128)}, f32[4,2048]{1,0:T(4,128)}, f32[4,2048]{1,0:T(4,128)}, bf16[4,4,16,8192]{3,2,1,0:T(8,128)(2,1)}) custom-call(f32[4,8192]{1,0:T(4,128)S(1)} %get-tuple-element.15.refs_0_, f32[4,8192]{1,0:T(4,128)S(1)} %get-tuple-element.16.refs_1_, f32[4,2048]{1,0:T(4,128)S(1)} %get-tuple-element.17.refs_2_, ...), custom_call_target="tpu_custom_call" | custom-call | tf_op jit(solution)/shard_map/write_out/pallas_call | solution.py:632
